TPU v7x, 256 devices: a whole 4x4x8 slice. The times are simulated.
256 devices in a mesh: panel: 2 (over z_hi), lat: 8 (over y, core), lon: 16 (over x, z_lo).
Axes of the slice: x: 4, y: 4, z: 8 (z_hi: 2, z_lo: 4; z = z_hi * 4 + z_lo), core: 2. Of those that a mesh axis runs over, the one named last changes fastest.
Arguments:
- tracers: float32 [2, 2, 36, 512, 2048], P('panel', None, None, 'lat', 'lon'), may hold values from -6 to 6
- winds: float32 [2, 2, 36, 512, 2048], P('panel', None, None, 'lat', 'lon'), may hold values from -0.3 to 0.3
- mixing: float32 [2, 35, 512, 2048], P('panel', None, 'lat', 'lon'), may hold values from 0.05 to 5
- strip_source: int32 [2, 320], replicated, may hold values from 0 to 127, as said below
- strip_tile: int32 [2, 320], replicated, may hold values from 0 to 127
- weights: bfloat16 [2, 320, 32, 64], replicated, may hold values from -1.5 to 1.5
Outputs:
- tracers_out: float32 [2, 2, 36, 512, 2048], P('panel', None, None, 'lat', 'lon')
Inputs may be any that keep to these rules, and one draw needn't show every extreme that they name: strip_source numbers a device of the other panel as its row of devices times (16) plus its column of devices. Strips 2m and 2m + 1 of a list have the same source device and lie on the same device; the pairs of strips that lie on one device come from distinct source devices. Over one panel's list, no device is named by more than 2 pairs of strips, and some device by exactly 2.
All inputs are finite; a program needn't handle non-finite values.
Results may differ from a plain program's by a relative error of at most 0.0003.
Values sent between devices are 32-bit elements; how exact they have to be, the bound alone decides.
A program may use at most 128 MiB of HBM per device.

v0:
```python
import jax
import jax.numpy as jnp
from jax import lax
from jax.sharding import PartitionSpec as P

STEPS = 2


SIXTH = 1.0 / 6.0


def with_halo(value, sides, width):
    for axis, dim in sides:
        peers, length = (lax.axis_size(axis), value.shape[dim])
        up = [(i, (i + 1) % peers) for i in range(peers - 1)]
        down = [(j, i) for i, j in up]
        last = lax.slice_in_dim(value, length - width, length, axis=dim)
        initial = lax.slice_in_dim(value, 0, width, axis=dim)
        before = lax.ppermute(last, axis, up)
        after = lax.ppermute(initial, axis, down)
        value = jnp.concatenate([before, value, after], axis=dim)
    return value


def from_partner(value, axis, stride):
    mask = 2**stride
    pairs = [(source, source ^ mask) for source in range(lax.axis_size(axis))]
    return lax.ppermute(value, axis, pairs)


def upwind_flux(courant, behind, upstream, downstream, beyond):
    rising = (5.0 * upstream + 2.0 * downstream - behind) * SIXTH
    falling = (2.0 * upstream + 5.0 * downstream - beyond) * SIXTH
    return jnp.maximum(courant, 0.0) * rising + jnp.minimum(courant, 0.0) * falling


def advect(padded, wind_pad):
    row_count = padded.shape[2] - 4
    col_count = padded.shape[3] - 4
    along_lon = padded[:, :, 2 : row_count + 2, :]
    east_wind = wind_pad[0, :, 1 : row_count + 1, :]
    face_east = 0.5 * (east_wind[:, :, 0 : col_count + 1] + east_wind[:, :, 1 : col_count + 2])
    flux_lon = upwind_flux(
        face_east,
        along_lon[..., 0 : col_count + 1],
        along_lon[..., 1 : col_count + 2],
        along_lon[..., 2 : col_count + 3],
        along_lon[..., 3 : col_count + 4],
    )
    along_lat = padded[:, :, :, 2 : col_count + 2]
    north_wind = wind_pad[1, :, :, 1 : col_count + 1]
    face_north = 0.5 * (north_wind[:, 0 : row_count + 1, :] + north_wind[:, 1 : row_count + 2, :])
    flux_lat = upwind_flux(
        face_north,
        along_lat[:, :, 0 : row_count + 1, :],
        along_lat[:, :, 1 : row_count + 2, :],
        along_lat[:, :, 2 : row_count + 3, :],
        along_lat[:, :, 3 : row_count + 4, :],
    )
    centre = padded[:, :, 2 : row_count + 2, 2 : col_count + 2]
    return (
        centre
        - (flux_lon[..., 1:] - flux_lon[..., :-1])
        - (flux_lat[:, :, 1:, :] - flux_lat[:, :, :-1, :])
    )


def diffuse(column_field, mixing):
    level_count = column_field.shape[1]
    ratios = []
    partial_vals = []
    for height in range(level_count):
        diagonal = 1.0 + jnp.zeros_like(mixing[0])
        source_term = column_field[:, height]
        if height > 0:
            diagonal = diagonal + mixing[height - 1]
        if height < level_count - 1:
            diagonal = diagonal + mixing[height]
        if height > 0:
            pivot_value = diagonal - mixing[height - 1] * ratios[-1]
            source_term = source_term + mixing[height - 1] * partial_vals[-1]
        else:
            pivot_value = diagonal
        partial_vals.append(source_term / pivot_value)
        if height < level_count - 1:
            ratios.append(mixing[height] / pivot_value)
    solved = [partial_vals[-1]]
    for height in range(level_count - 2, -1, -1):
        solved.insert(0, partial_vals[height] + ratios[height] * solved[0])
    return jnp.stack(solved, axis=1)


def slot_strips(lat_pos, lon_pos, lat_count, lon_count, across_count, down_count):
    across_band = lon_count * across_count
    down_band = lat_count * down_count
    across_steps = jnp.arange(across_count, dtype=jnp.int32)
    down_steps = jnp.arange(down_count, dtype=jnp.int32)
    north_ids = lon_pos * across_count + across_steps
    band_ids = jnp.where(lat_pos == 0, north_ids, north_ids + across_band)
    west_ids = 2 * across_band + lat_pos * down_count + down_steps
    side_ids = jnp.where(lon_pos == 0, west_ids, west_ids + down_band)
    return jnp.concatenate([band_ids, side_ids], axis=-1)


def on_device(tracers, winds, mixing, strip_source, strip_tile, weights):
    lat_count = lax.axis_size("lat")
    lon_count = lax.axis_size("lon")
    device_count = lat_count * lon_count
    panel_index = lax.axis_index("panel")
    lat_index = lax.axis_index("lat")
    lon_index = lax.axis_index("lon")
    own_flat = lat_index * lon_count + lon_index
    partner_panel = 1 - panel_index
    tracer_state = tracers[0]
    tracer_count, level_count, row_count, col_count = tracer_state.shape
    field_count = tracer_count * level_count
    across_count = col_count // 16
    down_count = row_count // 16
    slot_count = across_count + down_count
    pair_count = slot_count // 2
    tile_count = row_count // 4 * (col_count // 16)
    column_mixing = mixing[0]
    wind_pad = with_halo(winds[0], (("lat", 2), ("lon", 3)), 1)
    partner_source = lax.dynamic_index_in_dim(strip_source, partner_panel, 0, keepdims=False)
    partner_tile = lax.dynamic_index_in_dim(strip_tile, partner_panel, 0, keepdims=False)
    own_source = lax.dynamic_index_in_dim(strip_source, panel_index, 0, keepdims=False)
    dest_flat = jnp.arange(device_count, dtype=jnp.int32)[:, None]
    dest_lat = dest_flat // lon_count
    dest_lon = dest_flat % lon_count
    dest_ids = slot_strips(dest_lat, dest_lon, lat_count, lon_count, across_count, down_count)
    band_ok = (dest_lat == 0) | (dest_lat == lat_count - 1)
    side_ok = (dest_lon == 0) | (dest_lon == lon_count - 1)
    dest_valid = jnp.concatenate(
        [
            jnp.broadcast_to(band_ok, (device_count, across_count)),
            jnp.broadcast_to(side_ok, (device_count, down_count)),
        ],
        axis=-1,
    )
    served = jnp.where(dest_valid & (jnp.take(partner_source, dest_ids) == own_flat), 1, 0).astype(
        jnp.int32
    )
    pair_served = served.reshape(device_count, pair_count, 2)[:, :, 0]
    present = jnp.sum(pair_served, axis=1)
    dest_tile = jnp.sum(
        pair_served[:, :, None]
        * jnp.take(partner_tile, dest_ids).reshape(device_count, pair_count, 2),
        axis=1,
    )
    send_tile = dest_tile.reshape(-1)
    send_rows = jnp.repeat(present, 2).astype(jnp.float32)[:, None, None]
    send_slots = present.shape[0]
    own_ids = slot_strips(lat_index, lon_index, lat_count, lon_count, across_count, down_count)
    own_rows = jnp.take(own_source, own_ids) * 2 + jnp.arange(slot_count, dtype=jnp.int32) % 2
    own_weights = lax.dynamic_index_in_dim(weights, panel_index, 0, keepdims=False)
    own_slot_weights = jnp.take(own_weights, own_ids, axis=0).astype(jnp.float32)
    has_side = (lon_index == 0) | (lon_index == lon_count - 1)
    side_start = jnp.where(lon_index == 0, 0, col_count - 2).astype(jnp.int32)
    has_band = (lat_index == 0) | (lat_index == lat_count - 1)
    band_start = jnp.where(lat_index == 0, 0, row_count - 2).astype(jnp.int32)
    for step_number in range(STEPS):
        padded = with_halo(tracer_state, (("lat", 2), ("lon", 3)), 2)
        diffused = diffuse(advect(padded, wind_pad), column_mixing)
        tile_table = diffused.reshape(field_count, row_count // 4, 4, col_count // 16, 16)
        tile_table = tile_table.transpose(1, 3, 0, 2, 4).reshape(tile_count, field_count, 64)
        picked = jnp.take(tile_table, send_tile, axis=0)
        outgoing = picked * send_rows
        outgoing = outgoing.reshape(send_slots, 2, -1)
        crossed = from_partner(outgoing, "panel", 0)
        arrived = lax.all_to_all(crossed, ("lat", "lon"), split_axis=0, concat_axis=0, tiled=True)
        arrived = arrived.reshape(device_count * 2, -1)
        gathered = jnp.take(arrived, own_rows, axis=0)
        values = jnp.einsum(
            "rfk,rck->rfc",
            gathered.reshape(slot_count, field_count, 64),
            own_slot_weights,
            precision=lax.Precision.HIGHEST,
        )
        band_values = values[:across_count].reshape(across_count, tracer_count, level_count, 2, 16)
        band_values = band_values.transpose(1, 2, 3, 0, 4).reshape(
            tracer_count, level_count, 2, col_count
        )
        side_values = values[across_count:].reshape(down_count, tracer_count, level_count, 16, 2)
        side_values = side_values.transpose(1, 2, 0, 3, 4).reshape(
            tracer_count, level_count, row_count, 2
        )
        current = lax.dynamic_slice_in_dim(diffused, side_start, 2, axis=3)
        diffused = lax.dynamic_update_slice_in_dim(
            diffused, jnp.where(has_side, side_values, current), side_start, axis=3
        )
        current = lax.dynamic_slice_in_dim(diffused, band_start, 2, axis=2)
        tracer_state = lax.dynamic_update_slice_in_dim(
            diffused, jnp.where(has_band, band_values, current), band_start, axis=2
        )
    return tracer_state[None]


def solution(mesh):
    return jax.shard_map(
        on_device,
        mesh=mesh,
        in_specs=(
            P("panel", None, None, "lat", "lon"),
            P("panel", None, None, "lat", "lon"),
            P("panel", None, "lat", "lon"),
            P(),
            P(),
            P(),
        ),
        out_specs=P("panel", None, None, "lat", "lon"),
        check_vma=False,
    )
```

profile of v0, /device:TPU:1, one launch (start us, length us, event | category | flops | bytes accessed | tf_op | source)
XLA Modules:
  0.0 1086.1 jit_solution(9831256061395735806)
XLA Ops:
  1.9 4.6 collective-permute-start
  10.7 3.1 collective-permute-start.4
  23.0 9.5 gather_fusion.2
  34.1 9.5 gather_fusion.3
  50.8 3.2 fusion.208
  55.1 3.3 copy.548
  58.4 4.2 collective-permute-start.6
  62.5 3.3 copy.549
  67.1 3.8 maximum_multiply_fusion.1
  70.9 3.2 copy.550
  74.1 3.2 copy.551
  77.3 3.1 fusion.21
  80.4 3.1 maximum_multiply_fusion
  84.8 3.2 fusion.209
  88.0 3.3 copy.544
  91.3 4.6 collective-permute-start.2
  95.9 3.3 copy.546
  100.6 7.0 fusion.13
  107.6 3.3 copy.545
  110.9 3.3 copy.547
  114.2 5.6 maximum_maximum_fusion
  119.8 5.4 fusion.4
  125.5 4.1 fusion.18
  154.7 7.9 copy.557
  162.6 8.8 reshape.11813
  171.4 4.8 copy.558
  176.2 6.6 gather_fusion.4
  182.9 8.0 copy.559
  190.9 5.4 select_multiply_fusion.1
  196.3 9.6 copy.560
  205.9 9.5 reshape.11818
  215.4 6.0 collective-permute-start.8
  221.4 204.1 %collective-permute-done.8 = f32[128,2,4608]{2,1,0:T(2,128)} collective-permute-done((f32[128,2,4608]{2,1,0:T(2,128)}, f32[128,2,4608]{2,1,0:T(2,128)}, u32[]{:S(2)}, u32[]{:S(2)}) %collective-permute-start.8) | collective-permute-done | bytes 4718624 | tf_op jit(solution)/shard_map/ppermute | solution.py:28
  425.5 15.0 %all-to-all-start = ((f32[128,2,4608]{2,1,0:T(2,128)}), f32[128,2,4608]{2,1,0:T(2,128)}, u32[]{:S(2)}, u32[]{:S(2)}) async-start(f32[128,2,4608]{2,1,0:T(2,128)} %collective-permute-done.8), calls=%async_computation | async-start | bytes 9437184 | tf_op jit(solution)/shard_map/all_to_all | solution.py:170
  441.8 5.6 copy.561
  448.9 98.7 %all-to-all-done = f32[128,2,4608]{2,1,0:T(2,128)} async-done(((f32[128,2,4608]{2,1,0:T(2,128)}), f32[128,2,4608]{2,1,0:T(2,128)}, u32[]{:S(2)}, u32[]{:S(2)}) %all-to-all-start) | async-done | bytes 4718624 | tf_op jit(solution)/shard_map/all_to_all | solution.py:170
  547.6 6.5 reshape.11819
  554.1 3.1 gather_fusion.5
  558.1 3.3 copy.563
  561.4 3.0 bitcast_select_fusion.1
  564.5 12.5 %dynamic_update_slice.13 = f32[2,36,64,128]{3,2,1,0:T(8,128)} dynamic-update-slice(f32[2,36,64,128]{3,2,1,0:T(8,128)} %constant_dynamic-update-slice_fusion, f32[2,36,64,2]{3,2,1,0:T(8,128)S(1)} %bitcast_select_fusion.1, s32[]{:T(128)} %constant.116.clone.1, s32[]{:T(128)} %constant.116.clone.1, s32[]{:T(128)} %constant.116.clone.1, s32[]{:T(128)S(6)} %select_n.212) | dynamic-update-slice | bytes 73732 | tf_op jit(solution)/shard_map/dynamic_update_slice | solution.py:188
  582.3 3.3 collective-permute-start.9
  589.0 3.2 fusion.207
  595.0 12.7 %collective-permute-start.11 = (f32[2,36,68,2]{2,3,1,0:T(2,128)S(1)}, f32[2,36,68,2]{2,3,1,0:T(2,128)S(1)}, u32[]{:S(2)}, u32[]{:S(2)}) collective-permute-start(f32[2,36,68,2]{2,3,1,0:T(2,128)S(1)} %copy.566), channel_id=1, source_target_pairs={{0,1},{1,2},{2,3},{3,4},{4,5},{5,6},{6,7},{7,8},{8,9},{9,10},{10,1... | collective-permute-start | bytes 117512 | tf_op jit(solution)/shard_map/ppermute | solution.py:19
  611.8 6.3 fusion.8
  620.6 3.4 copy.569
  624.0 5.7 maximum_maximum_fusion.1
  629.7 3.9 fusion.1
  661.8 7.9 copy.570
  669.6 8.8 reshape.11825
  678.5 4.8 copy.571
  683.3 6.6 gather_fusion.6
  689.9 8.0 copy.572
  698.0 5.4 select_multiply_fusion
  703.4 9.4 copy.573
  712.7 9.5 reshape.11827
  724.6 106.2 %collective-permute-done.13 = f32[128,2,4608]{2,1,0:T(2,128)S(1)} collective-permute-done((f32[128,2,4608]{2,1,0:T(2,128)}, f32[128,2,4608]{2,1,0:T(2,128)S(1)}, u32[]{:S(2)}, u32[]{:S(2)}) %collective-permute-start.13) | collective-permute-done | bytes 4718624 | tf_op jit(solution)/shard_map/ppermute | solution.py:28
  830.9 218.4 %all_to_all.10 = f32[128,2,4608]{2,1,0:T(2,128)} all-to-all(f32[128,2,4608]{2,1,0:T(2,128)S(1)} %collective-permute-done.13), channel_id=1, replica_groups=mesh['panel'=2,'lat'=8,'lon'=16] {'lat','lon'}, dimensions={0} | all-to-all | bytes 9437184 | tf_op jit(solution)/shard_map/all_to_all | solution.py:170
  1049.3 6.5 reshape.11828
  1055.8 3.1 gather_fusion.7
  1059.7 3.4 copy.575
  1063.1 3.0 bitcast_select_fusion
  1066.2 12.5 %dynamic_update_slice.15 = f32[2,36,64,128]{3,2,1,0:T(8,128)} dynamic-update-slice(f32[2,36,64,128]{3,2,1,0:T(8,128)} %constant_dynamic-update-slice_fusion.36, f32[2,36,64,2]{3,2,1,0:T(8,128)S(1)} %bitcast_select_fusion, s32[]{:T(128)} %constant.116.clone.1, s32[]{:T(128)} %constant.116.clone.1, s32[]{:T(128)} %constant.116.clone.1, s32[]{:T(128)S(6)} %select_n.212) | dynamic-update-slice | bytes 73732 | tf_op jit(solution)/shard_map/dynamic_update_slice | solution.py:188
  1078.7 3.5 copy.656
  (346 shorter events, 110.2 us)
Async XLA Ops:
  0.0 440.5 %copy-start = (bf16[2,320,32,64]{1,3,2,0:T(8,128)(2,1)S(1)}, bf16[2,320,32,64]{1,3,2,0:T(8,128)(2,1)}, u32[]{:S(2)}) copy-start(bf16[2,320,32,64]{1,3,2,0:T(8,128)(2,1)} %param.17) | copy-start | bytes 7864324
  0.0 18.4 %copy-start.12 = (f32[1,35,64,128]{3,2,1,0:T(8,128)S(1)}, f32[1,35,64,128]{3,2,1,0:T(8,128)}, u32[]{:S(2)}) copy-start(f32[1,35,64,128]{3,2,1,0:T(8,128)} %param.14) | copy-start | bytes 3440644
  1.9 81.5 %collective-permute-start = (f32[2,36,2,128]{3,2,1,0:T(2,128)}, f32[2,36,2,128]{3,2,1,0:T(2,128)}, u32[]{:S(2)}, u32[]{:S(2)}) collective-permute-start(f32[2,36,2,128]{3,2,1,0:T(2,128)} %get-tuple-element.168), channel_id=1, source_target_pairs={{0,16},{16,32},{32,48},{48,64},{64,80},{80,96},{96,112},{1,17},{17... | collective-permute-start | bytes 221192 | tf_op jit(solution)/shard_map/ppermute | solution.py:19
  6.5 77.0 %collective-permute-start.1 = (f32[2,36,2,128]{3,2,1,0:T(2,128)}, f32[2,36,2,128]{3,2,1,0:T(2,128)}, u32[]{:S(2)}, u32[]{:S(2)}) collective-permute-start(f32[2,36,2,128]{3,2,1,0:T(2,128)} %get-tuple-element.169), channel_id=1, source_target_pairs={{16,0},{32,16},{48,32},{64,48},{80,64},{96,80},{112,96},{17,1},{33... | collective-permute-start | bytes 221192 | tf_op jit(solution)/shard_map/ppermute | solution.py:20
  10.7 38.1 %collective-permute-start.4 = (f32[2,36,1,128]{3,2,1,0:T(1,128)}, f32[2,36,1,128]{3,2,1,0:T(1,128)}, u32[]{:S(2)}, u32[]{:S(2)}) collective-permute-start(f32[2,36,1,128]{3,2,1,0:T(1,128)} %get-tuple-element.166), channel_id=1, source_target_pairs={{0,16},{16,32},{32,48},{48,64},{64,80},{80,96},{96,112},{1,17},{17... | collective-permute-start | bytes 110600 | tf_op jit(solution)/shard_map/ppermute | solution.py:19
  13.8 9.1 copy-start.86
  13.8 9.1 copy-start.87
  13.8 35.0 %collective-permute-start.5 = (f32[2,36,1,128]{3,2,1,0:T(1,128)}, f32[2,36,1,128]{3,2,1,0:T(1,128)}, u32[]{:S(2)}, u32[]{:S(2)}) collective-permute-start(f32[2,36,1,128]{3,2,1,0:T(1,128)} %get-tuple-element.167), channel_id=1, source_target_pairs={{16,0},{32,16},{48,32},{64,48},{80,64},{96,80},{112,96},{17,1},{33... | collective-permute-start | bytes 110600 | tf_op jit(solution)/shard_map/ppermute | solution.py:20
  34.1 11.1 %copy-start.88 = (pred[128]{0:T(512)(128)(4,1)S(1)}, pred[128]{0:T(512)(128)(4,1)}, u32[]{:S(2)}) copy-start(pred[128]{0:T(512)(128)(4,1)} %get-tuple-element.213) | copy-start | bytes 388
  58.4 12.5 %collective-permute-start.6 = (f32[2,36,66,1]{2,0,3,1:T(2,128)}, f32[2,36,66,1]{2,0,3,1:T(2,128)}, u32[]{:S(2)}, u32[]{:S(2)}) collective-permute-start(f32[2,36,66,1]{2,0,3,1:T(2,128)} %copy.548), channel_id=1, source_target_pairs={{0,1},{1,2},{2,3},{3,4},{4,5},{5,6},{6,7},{7,8},{8,9},{9,10},{10,1... | collective-permute-start | bytes 57032 | tf_op jit(solution)/shard_map/ppermute | solution.py:19
  65.8 8.2 collective-permute-start.7
  91.3 16.3 %collective-permute-start.2 = (f32[2,36,68,2]{2,3,1,0:T(2,128)}, f32[2,36,68,2]{2,3,1,0:T(2,128)}, u32[]{:S(2)}, u32[]{:S(2)}) collective-permute-start(f32[2,36,68,2]{2,3,1,0:T(2,128)} %copy.544), channel_id=1, source_target_pairs={{0,1},{1,2},{2,3},{3,4},{4,5},{5,6},{6,7},{7,8},{8,9},{9,10},{10,1... | collective-permute-start | bytes 117512 | tf_op jit(solution)/shard_map/ppermute | solution.py:19
  99.1 11.7 %collective-permute-start.3 = (f32[2,36,68,2]{2,3,1,0:T(2,128)}, f32[2,36,68,2]{2,3,1,0:T(2,128)}, u32[]{:S(2)}, u32[]{:S(2)}) collective-permute-start(f32[2,36,68,2]{2,3,1,0:T(2,128)} %copy.546), channel_id=1, source_target_pairs={{1,0},{2,1},{3,2},{4,3},{5,4},{6,5},{7,6},{8,7},{9,8},{10,9},{11,1... | collective-permute-start | bytes 117512 | tf_op jit(solution)/shard_map/ppermute | solution.py:20
  114.2 5.6 copy-start.4
  114.2 5.6 copy-start.6
  119.8 5.4 copy-start.3
  119.8 5.4 copy-start.9
  125.1 4.4 copy-start.15
  125.2 4.4 copy-start.17
  125.2 4.4 copy-start.19
  125.2 4.4 copy-start.21
  125.2 4.4 copy-start.23
  125.2 4.4 copy-start.25
  125.2 4.4 copy-start.27
  125.2 4.4 copy-start.30
  125.2 4.4 copy-start.32
  125.2 4.4 copy-start.34
  125.2 4.4 copy-start.36
  125.2 4.4 copy-start.38
  125.3 4.4 copy-start.40
  125.3 4.4 copy-start.42
  125.3 4.4 copy-start.44
  125.3 4.4 copy-start.46
  125.3 4.4 copy-start.48
  125.3 4.4 copy-start.50
  125.3 4.4 copy-start.52
  125.3 4.4 copy-start.54
  125.3 4.4 copy-start.56
  125.3 4.4 copy-start.58
  125.4 4.4 copy-start.60
  125.4 4.4 copy-start.62
  125.4 4.4 copy-start.64
  125.4 4.4 copy-start.66
  125.4 4.4 copy-start.68
  125.4 4.4 copy-start.70
  125.4 4.4 copy-start.72
  125.4 4.4 copy-start.74
  125.4 4.4 copy-start.76
  125.5 4.4 copy-start.78
  125.5 4.4 copy-start.80
  125.5 4.4 copy-start.82
  215.4 210.1 %collective-permute-start.8 = (f32[128,2,4608]{2,1,0:T(2,128)}, f32[128,2,4608]{2,1,0:T(2,128)}, u32[]{:S(2)}, u32[]{:S(2)}) collective-permute-start(f32[128,2,4608]{2,1,0:T(2,128)} %reshape.11818), channel_id=1, source_target_pairs={{0,128},{128,0},{1,129},{129,1},{2,130},{130,2},{3,131},{131,3},{4... | collective-permute-start | bytes 14155784 | tf_op jit(solution)/shard_map/ppermute | solution.py:28
  425.5 122.1 %all-to-all-start = ((f32[128,2,4608]{2,1,0:T(2,128)}), f32[128,2,4608]{2,1,0:T(2,128)}, u32[]{:S(2)}, u32[]{:S(2)}) async-start(f32[128,2,4608]{2,1,0:T(2,128)} %collective-permute-done.8), calls=%async_computation | async-start | bytes 9437184 | tf_op jit(solution)/shard_map/all_to_all | solution.py:170
  580.0 5.7 collective-permute-start.10
  582.3 4.7 collective-permute-start.9
  592.2 19.6 %copy-start.10 = (f32[36,65,128]{2,1,0:T(8,128)S(1)}, f32[36,65,128]{2,1,0:T(8,128)}, u32[]{:S(2)}) copy-start(f32[36,65,128]{2,1,0:T(8,128)} %get-tuple-element.170) | copy-start | bytes 3594244
  592.2 19.6 %copy-start.11 = (f32[36,65,128]{2,1,0:T(8,128)S(1)}, f32[36,65,128]{2,1,0:T(8,128)}, u32[]{:S(2)}) copy-start(f32[36,65,128]{2,1,0:T(8,128)} %get-tuple-element.171) | copy-start | bytes 3594244
  595.0 23.1 %collective-permute-start.11 = (f32[2,36,68,2]{2,3,1,0:T(2,128)S(1)}, f32[2,36,68,2]{2,3,1,0:T(2,128)S(1)}, u32[]{:S(2)}, u32[]{:S(2)}) collective-permute-start(f32[2,36,68,2]{2,3,1,0:T(2,128)S(1)} %copy.566), channel_id=1, source_target_pairs={{0,1},{1,2},{2,3},{3,4},{4,5},{5,6},{6,7},{7,8},{8,9},{9,10},{10,1... | collective-permute-start | bytes 117512 | tf_op jit(solution)/shard_map/ppermute | solution.py:19
  610.3 10.3 collective-permute-start.12
  624.0 5.7 copy-start.5
  624.0 5.7 copy-start.7
  722.3 108.6 %collective-permute-start.13 = (f32[128,2,4608]{2,1,0:T(2,128)}, f32[128,2,4608]{2,1,0:T(2,128)S(1)}, u32[]{:S(2)}, u32[]{:S(2)}) collective-permute-start(f32[128,2,4608]{2,1,0:T(2,128)} %reshape.11827), channel_id=1, source_target_pairs={{0,128},{128,0},{1,129},{129,1},{2,130},{130,2},{3,131},{131,3},{4... | collective-permute-start | bytes 14155784 | tf_op jit(solution)/shard_map/ppermute | solution.py:28
  1059.6 6.6 copy-start.29
  1078.7 7.2 copy-start.1
  (41 other events, 124.8 us)
where the time goes:
time: 1110 us; the launch traced here: 1090 us
  waiting for transfers between devices  410 us (37%)
  local copies, waits for them, and re-layouts  279 us (25%)
  blocking collectives  218 us (20%)
  other arithmetic  109 us (10%)
  starting transfers between devices  66.6 us (6%)
    ppermute x2, waiting for transfers between devices, from_partner(): return lax.ppermute(value, axis, pairs)  310 us
    all_to_all x1, blocking collectives, on_device(): lax.all_to_all(crossed, ('lat', 'lon'), split_axis=0, concat_axis=0, tile...  218 us
    all_to_all x1, waiting for transfers between devices, on_device(): lax.all_to_all(crossed, ('lat', 'lon'), split_axis=0, concat_axis=0, tile...  98.7 us
    ppermute x6, starting transfers between devices, with_halo(): before = lax.ppermute(last, axis, up)  32.4 us
    gather x4, local copies, waits for them, and re-layouts, on_device(): picked = jnp.take(tile_table, send_tile, axis=0)  29.4 us
    unnamed x36, other arithmetic  27.1 us
    unnamed x214, local copies, waits for them, and re-layouts  25.1 us
    dynamic_update_slice x2, local copies, waits for them, and re-layouts, on_device(): lax.dynamic_update_slice_in_dim(diffused, jnp.where(has_side, side_values...  25 us
  transfers between devices with their start and end apart: 15, of which 5 were waited for; matrix products, arithmetic and copies ran while one was open for 9% of the time, Pallas kernels for 0%

commit v1 on v0

v1 whole, which is shorter than its diff:
```python
import functools

import jax
import jax.numpy as jnp
from jax import lax
from jax.experimental import pallas as pl
from jax.experimental.pallas import tpu as pltpu
from jax.sharding import PartitionSpec as P

MESH = pl.DeviceIdType.MESH
STEPS = 2
MIDS = 18
FIELDS = 72
LEVELS = 36
ROWS = 64
COLS = 128
SHARE = FIELDS // MIDS
PAD = 8
TALL = ROWS + 2 * PAD
CHUNK = 16
EAST, WEST, SOUTH, NORTH = range(4)


def mid_place(k):
    return 1 + k % 6, 1 + (5 * k) % 14


def kernel(lat_n, lon_n, tab, info, tr_hbm, wd_hbm, mix_hbm, wt_hbm, out_hbm,
           sa, sb, w0, w1, mx, cf, rt, wts, bd, pk, pkr, hp, rw, rwr, prev,
           pay, inb0, inb1, ob, rb, rs, dense, flip,
           lsem, ssem, rsem, p1s, p1r, p2s, p2bs, p2r, p2br):
    panel = lax.axis_index("panel")
    lat = lax.axis_index("lat")
    lon = lax.axis_index("lon")
    me = lat * lon_n + lon
    other = 1 - panel
    has = {
        EAST: lon < lon_n - 1,
        WEST: lon > 0,
        SOUTH: lat < lat_n - 1,
        NORTH: lat > 0,
    }
    beside = {
        EAST: (panel, lat, lon + 1),
        WEST: (panel, lat, lon - 1),
        SOUTH: (panel, lat + 1, lon),
        NORTH: (panel, lat - 1, lon),
    }
    is_band = (lat == 0) | (lat == lat_n - 1)
    is_side = (lon == 0) | (lon == lon_n - 1)
    mid_id = jnp.int32(-1)
    for k in range(MIDS):
        mlat, mlon = mid_place(k)
        mid_id = jnp.where((lat == mlat) & (lon == mlon), jnp.int32(k), mid_id)
    is_mid = mid_id >= 0
    inb = (inb0, inb1)
    lane8 = lax.broadcasted_iota(jnp.int32, (8, COLS), 1)
    lane_c = lax.broadcasted_iota(jnp.int32, (CHUNK, COLS), 1)

    loads = [
        pltpu.make_async_copy(tr_hbm, sa.at[:, pl.ds(PAD, ROWS), :], lsem.at[0]),
        pltpu.make_async_copy(wd_hbm.at[0], w0, lsem.at[1]),
        pltpu.make_async_copy(wd_hbm.at[1], w1.at[:, pl.ds(PAD, ROWS), :], lsem.at[2]),
        pltpu.make_async_copy(mix_hbm, mx.at[pl.ds(1, LEVELS - 1)], lsem.at[3]),
        pltpu.make_async_copy(wt_hbm.at[other], wts, lsem.at[4]),
    ]
    for load in loads:
        load.start()

    barrier = pltpu.get_barrier_semaphore()
    for way in range(4):
        @pl.when(has[way])
        def _():
            pl.semaphore_signal(barrier, inc=1, device_id=beside[way], device_id_type=MESH)

    @pl.when(is_mid)
    def _():
        def greet(i, carry):
            pl.semaphore_signal(
                barrier, inc=1, device_id=(other, i // lon_n, i % lon_n), device_id_type=MESH)
            return carry
        lax.fori_loop(0, lat_n * lon_n, greet, 0)

    def greet_mids():
        def greet(k, carry):
            mlat, mlon = mid_place(k)
            pl.semaphore_signal(
                barrier, inc=1, device_id=(panel, mlat, mlon), device_id_type=MESH)
            return carry
        lax.fori_loop(0, MIDS, greet, 0)

    pl.when(is_band)(greet_mids)
    pl.when(is_side)(greet_mids)
    one = jnp.int32(1)
    none = jnp.int32(0)
    expect = jnp.int32(MIDS)
    for way in range(4):
        expect = expect + jnp.where(has[way], one, none)
    expect = expect + jnp.where(is_mid, jnp.int32(2 * lon_n + 2 * lat_n), none)

    zero = jnp.zeros((ROWS, COLS), jnp.float32)
    mx[0] = zero
    mx[LEVELS] = zero
    rt[0] = zero
    bd[...] = jnp.zeros((128, 256), jnp.float32)
    for step in range(STEPS):
        for way in range(2):
            @pl.when(jnp.logical_not(has[way ^ 1]))
            def _():
                pkr[step, way] = jnp.zeros((4, ROWS, COLS), jnp.float32)

            @pl.when(jnp.logical_not(has[2 + (way ^ 1)]))
            def _():
                rwr[step, way] = jnp.zeros((FIELDS + LEVELS, 2, COLS), jnp.float32)
    loads[0].wait()
    loads[1].wait()
    loads[2].wait()

    def halo_copy(step, way):
        groups = 4 if step == 0 else 3
        fields = FIELDS + LEVELS if step == 0 else FIELDS
        if way in (EAST, WEST):
            src = pk.at[step, pl.ds(0, groups)]
            dst = pkr.at[step, way, pl.ds(0, groups)]
        else:
            src = rw.at[step, way - 2, pl.ds(0, fields)]
            dst = rwr.at[step, way - 2, pl.ds(0, fields)]
        return pltpu.make_async_remote_copy(
            src_ref=src, dst_ref=dst, send_sem=ssem.at[step, way], recv_sem=rsem.at[step, way],
            device_id=beside[way], device_id_type=MESH)

    def exchange(step, state):
        def pack(g, carry):
            rows = pl.ds(pl.multiple_of(PAD + g * 8, 8), 8)
            bare = pl.ds(pl.multiple_of(g * 8, 8), 8)
            count = FIELDS + LEVELS if step == 0 else FIELDS
            for group in range((count + 31) // 32):
                total = jnp.zeros((8, COLS), jnp.float32)
                for slot in range(min(32, count - 32 * group)):
                    f = 32 * group + slot
                    value = state[f, rows, :] if f < FIELDS else w0[f - FIELDS, bare, :]
                    moved = pltpu.roll(value, (4 * slot + 2) % COLS, 1)
                    total = jnp.where(lane8 // 4 == slot, moved, total)
                pk[step, group, bare, :] = total
            return carry
        lax.fori_loop(0, ROWS // 8, pack, 0)

        def rows_of(f, carry):
            rw[step, 0, f] = state[f, PAD + ROWS - 2:PAD + ROWS, :]
            rw[step, 1, f] = state[f, PAD:PAD + 2, :]
            return carry
        lax.fori_loop(0, FIELDS, rows_of, 0, unroll=8)
        if step == 0:
            def winds_of(l, carry):
                rw[step, 0, FIELDS + l] = w1[l, PAD + ROWS - 2:PAD + ROWS, :]
                rw[step, 1, FIELDS + l] = w1[l, PAD:PAD + 2, :]
                return carry
            lax.fori_loop(0, LEVELS, winds_of, 0, unroll=4)
            pl.semaphore_wait(barrier, expect)
        for way in range(4):
            @pl.when(has[way])
            def _():
                halo_copy(step, way).start()

    def take_halo(step, state):
        for way, came in ((EAST, WEST), (WEST, EAST), (SOUTH, NORTH), (NORTH, SOUTH)):
            @pl.when(has[came])
            def _():
                halo_copy(step, way).wait_recv()
        for group in range(4 if step == 0 else 3):
            for g in range(ROWS // CHUNK):
                rows = pl.ds(g * CHUNK, CHUNK)
                hp[group, rows, :] = jnp.where(
                    lane_c % 4 < 2, pkr[step, EAST, group, rows, :], pkr[step, WEST, group, rows, :])

        def rows_of(f, carry):
            state[f, PAD - 2:PAD, :] = rwr[step, 0, f]
            state[f, PAD + ROWS:PAD + ROWS + 2, :] = rwr[step, 1, f]
            return carry
        lax.fori_loop(0, FIELDS, rows_of, 0, unroll=8)
        if step == 0:
            def winds_of(l, carry):
                w1[l, PAD - 2:PAD, :] = rwr[step, 0, FIELDS + l]
                w1[l, PAD + ROWS:PAD + ROWS + 2, :] = rwr[step, 1, FIELDS + l]
                return carry
            lax.fori_loop(0, LEVELS, winds_of, 0, unroll=4)

    def sent_halo(step):
        for way in range(4):
            @pl.when(has[way])
            def _():
                halo_copy(step, way).wait_send()

    def halo_lanes(f, g):
        slot = f % 32
        return pltpu.roll(
            hp[f // 32, pl.ds(g * CHUNK, CHUNK), :], (2 * COLS - 2 - 4 * slot) % COLS, 1)

    def coefficients(l, carry):
        for g in range(ROWS // CHUNK):
            rows = pl.ds(g * CHUNK, CHUNK)
            w = w0[l, rows, :]
            beyond = halo_lanes(FIELDS + l, g)
            w_east = pltpu.roll(jnp.where(lane_c < 1, beyond, w), COLS - 1, 1)
            w_west = pltpu.roll(jnp.where(lane_c >= COLS - 1, beyond, w), 1, 1)
            base = PAD + g * CHUNK
            v = w1[l, base:base + CHUNK, :]
            v_next = w1[l, base + 1:base + CHUNK + 1, :]
            v_prev = w1[l, base - 1:base + CHUNK - 1, :]

            def parts(face):
                face = face * (1.0 / 12.0)
                return jnp.maximum(face, 0.0), jnp.minimum(face, 0.0)

            pe, me_ = parts(w + w_east)
            pw, mw = parts(w + w_west)
            pn, mn = parts(v + v_next)
            ps, ms = parts(v + v_prev)
            low = mx[l, rows, :]
            high = mx[l + 1, rows, :]
            pivot = 1.0 + low + high - low * rt[l, rows, :]
            inv = 1.0 / pivot
            rt[l + 1, rows, :] = high * inv
            centre = 1.0 + (2.0 * (pw - me_) + 5.0 * (mw - pe)) + (2.0 * (ps - mn) + 5.0 * (ms - pn))
            for i, c in enumerate((
                centre,
                -pw, 5.0 * pw + 2.0 * mw + pe, -mw - 2.0 * pe - 5.0 * me_, me_,
                -ps, 5.0 * ps + 2.0 * ms + pn, -ms - 2.0 * pn - 5.0 * mn, mn,
                low,
            )):
                cf[l, i, rows, :] = c * inv
        return carry

    def forward(state, new):
        prev[...] = jnp.zeros((2, ROWS, COLS), jnp.float32)

        def level(l, carry):
            for g in range(ROWS // CHUNK):
                rows = pl.ds(g * CHUNK, CHUNK)
                base = PAD + g * CHUNK
                for t in range(2):
                    f = t * LEVELS + l
                    q = state[f, base:base + CHUNK, :]
                    beyond = halo_lanes(f, g)
                    x = cf[l, 0, rows, :] * q
                    x += cf[l, 1, rows, :] * pltpu.roll(jnp.where(lane_c >= COLS - 2, beyond, q), 2, 1)
                    x += cf[l, 2, rows, :] * pltpu.roll(jnp.where(lane_c >= COLS - 1, beyond, q), 1, 1)
                    x += cf[l, 3, rows, :] * pltpu.roll(jnp.where(lane_c < 1, beyond, q), COLS - 1, 1)
                    x += cf[l, 4, rows, :] * pltpu.roll(jnp.where(lane_c < 2, beyond, q), COLS - 2, 1)
                    x += cf[l, 5, rows, :] * state[f, base - 2:base - 2 + CHUNK, :]
                    x += cf[l, 6, rows, :] * state[f, base - 1:base - 1 + CHUNK, :]
                    x += cf[l, 7, rows, :] * state[f, base + 1:base + 1 + CHUNK, :]
                    x += cf[l, 8, rows, :] * state[f, base + 2:base + 2 + CHUNK, :]
                    x += cf[l, 9, rows, :] * prev[t, rows, :]
                    prev[t, rows, :] = x
                    new[f, base:base + CHUNK, :] = x
            return carry
        lax.fori_loop(0, LEVELS, level, 0)

    def backward(new):
        def level(i, carry):
            l = LEVELS - 2 - i
            for g in range(ROWS // CHUNK):
                rows = pl.ds(g * CHUNK, CHUNK)
                base = PAD + g * CHUNK
                for t in range(2):
                    f = t * LEVELS + l
                    x = new[f, base:base + CHUNK, :] + rt[l + 1, rows, :] * prev[t, rows, :]
                    prev[t, rows, :] = x
                    new[f, base:base + CHUNK, :] = x
            return carry
        lax.fori_loop(0, LEVELS - 1, level, 0)

    def to_mid(step, k):
        mlat, mlon = mid_place(k)
        return pltpu.make_async_remote_copy(
            src_ref=pay.at[step, k], dst_ref=inb[step].at[me], send_sem=p1s.at[step],
            recv_sem=p1r.at[step], device_id=(other, mlat, mlon), device_id_type=MESH)

    def to_band(step, d):
        return pltpu.make_async_remote_copy(
            src_ref=ob.at[step, pl.ds(2 * d, 2)], dst_ref=rb.at[step, mid_id],
            send_sem=p2bs.at[step], recv_sem=p2br.at[step],
            device_id=(panel, (d // lon_n) * (lat_n - 1), d % lon_n), device_id_type=MESH)

    def to_side(step, e):
        return pltpu.make_async_remote_copy(
            src_ref=ob.at[step, 4 * lon_n + e], dst_ref=rs.at[step, mid_id],
            send_sem=p2s.at[step], recv_sem=p2r.at[step],
            device_id=(panel, e % lat_n, (e // lat_n) * (lon_n - 1)), device_id_type=MESH)

    def all_of(ref, sem):
        pltpu.make_async_copy(ref, ref, sem).wait()

    def provide(step, new):
        flat = new.reshape(FIELDS * TALL, COLS)
        lane_f = lax.broadcasted_iota(jnp.int32, (FIELDS, COLS), 1)
        total = jnp.zeros((FIELDS, COLS), jnp.float32)
        for pair in range(2):
            cells = jnp.zeros((FIELDS, COLS), jnp.float32)
            for s in range(2):
                tile = info[2 + 2 * pair + s]
                first = PAD + (tile // 8) * 4
                for r in range(4):
                    row = flat[pl.ds(first + r, FIELDS, stride=TALL), :]
                    shift = (2 * COLS + 64 * s + 16 * r - 16 * (tile % 8)) % COLS
                    row = pltpu.roll(row, shift, 1)
                    cells = jnp.where(lane_f // 16 == 4 * s + r, row, cells)
            w = bd[:, 128 * pair:128 * pair + 128].astype(jnp.bfloat16)
            rest = cells
            for part in range(3):
                piece = rest.astype(jnp.bfloat16)
                total += lax.dot_general(
                    piece, w, (((1,), (1,)), ((), ())), preferred_element_type=jnp.float32)
                if part < 2:
                    rest = rest - piece.astype(jnp.float32)
        for k in range(MIDS):
            pay[step, k] = total[SHARE * k:SHARE * k + SHARE, :]

        def send(k, carry):
            to_mid(step, k).start()
            return carry
        lax.fori_loop(0, MIDS, send, 0)

        @pl.when(is_mid)
        def _():
            all_of(inb[step], p1r.at[step])
            lane_s = lax.broadcasted_iota(jnp.int32, (SHARE, COLS), 1)
            batch = 8

            def sort(i, carry):
                done = []
                for j in range(batch):
                    u = i * batch + j
                    left = tab[2 * u]
                    right = tab[2 * u + 1]
                    a = pltpu.roll(inb[step][left // 2], (left % 2) * 64, 1)
                    b = pltpu.roll(inb[step][right // 2], 64 - (right % 2) * 64, 1)
                    done.append(jnp.where(lane_s < 64, a, b))
                for j in range(batch):
                    ob[step, i * batch + j] = done[j]
                return carry
            lax.fori_loop(0, (4 * lon_n + 2 * lat_n) // batch, sort, 0)

            def band(d, carry):
                to_band(step, d).start()
                return carry
            lax.fori_loop(0, 2 * lon_n, band, 0)

            def side(e, carry):
                to_side(step, e).start()
                return carry
            lax.fori_loop(0, 2 * lat_n, side, 0)

    def fill(step, new):
        @pl.when(is_side)
        def _():
            all_of(rs.at[step], p2r.at[step])
            for k in range(MIDS):
                dense[0, SHARE * k:SHARE * k + SHARE, :] = rs[step, k]
            flip[...] = jnp.transpose(dense[0])
            first = flip[pl.ds(0, ROWS, stride=2), :]
            second = flip[pl.ds(1, ROWS, stride=2), :]
            dense[0, 0:ROWS, :] = first
            dense[1, 0:ROWS, :] = second
            start = jnp.where(lon == 0, 0, COLS - 2)

            def column(f, carry):
                for g in range(ROWS // CHUNK):
                    rows = pl.ds(g * CHUNK, CHUNK)
                    base = PAD + g * CHUNK
                    a = pltpu.roll(dense[0, rows, :], (COLS + start - f) % COLS, 1)
                    b = pltpu.roll(dense[1, rows, :], (COLS + start + 1 - f) % COLS, 1)
                    q = new[f, base:base + CHUNK, :]
                    q = jnp.where(lane_c == start, a, q)
                    new[f, base:base + CHUNK, :] = jnp.where(lane_c == start + 1, b, q)
                return carry
            lax.fori_loop(0, FIELDS, column, 0, unroll=2)

        @pl.when(is_band)
        def _():
            all_of(rb.at[step], p2br.at[step])
            for k in range(MIDS):
                for u in range(2):
                    dense[u, SHARE * k:SHARE * k + SHARE, :] = rb[step, k, u]
            lane_f = lax.broadcasted_iota(jnp.int32, (FIELDS, COLS), 1)
            lines = []
            for r in range(2):
                line = jnp.zeros((FIELDS, COLS), jnp.float32)
                for u in range(2):
                    tiles = dense[u, 0:FIELDS, :]
                    for s in range(4):
                        moved = pltpu.roll(tiles, (2 * COLS + 64 * u - 16 * s - 16 * r) % COLS, 1)
                        line = jnp.where(lane_f // 16 == 4 * u + s, moved, line)
                lines.append(line)
            flat = new.reshape(FIELDS * TALL, COLS)
            for r in range(2):
                @pl.when(lat == 0)
                def _():
                    flat[pl.ds(PAD + r, FIELDS, stride=TALL), :] = lines[r]

                @pl.when(lat == lat_n - 1)
                def _():
                    flat[pl.ds(PAD + ROWS - 2 + r, FIELDS, stride=TALL), :] = lines[r]

    for step in range(STEPS):
        state, new = (sa, sb) if step % 2 == 0 else (sb, sa)
        exchange(step, state)
        if step == 0:
            loads[4].wait()
            for pair in range(2):
                for s in range(2):
                    b = 2 * pair + s
                    bd[32 * b:32 * b + 32, 64 * b:64 * b + 64] = wts[
                        2 * info[pair] + s].astype(jnp.float32)
            loads[3].wait()
        take_halo(step, state)
        if step == 0:
            lax.fori_loop(0, LEVELS, coefficients, 0)
        forward(state, new)
        backward(new)
        provide(step, new)
        fill(step, new)

    result = sa if STEPS % 2 == 0 else sb
    store = pltpu.make_async_copy(result.at[:, pl.ds(PAD, ROWS), :], out_hbm, lsem.at[0])
    store.start()
    for step in range(STEPS):
        sent_halo(step)
        all_of(pay.at[step], p1s.at[step])

        @pl.when(is_mid)
        def _():
            all_of(ob.at[step, pl.ds(0, 4 * lon_n)], p2bs.at[step])
            all_of(ob.at[step, pl.ds(4 * lon_n, 2 * lat_n)], p2s.at[step])
    store.wait()


def on_device(lat_n, lon_n, tracers, winds, mixing, strip_source, strip_tile, weights):
    panel = lax.axis_index("panel")
    me = lax.axis_index("lat") * lon_n + lax.axis_index("lon")
    sources = strip_source[:, ::2]
    pairs = sources.shape[1]
    order = jnp.arange(pairs, dtype=jnp.int32)
    same = (sources[:, :, None] == sources[:, None, :]) & (order[None, :] < order[:, None])[None]
    second = jnp.any(same, axis=2).astype(jnp.int32)
    tab = lax.dynamic_index_in_dim(sources * 2 + second, panel, 0, keepdims=False)
    theirs = lax.dynamic_index_in_dim(sources, 1 - panel, 0, keepdims=False)
    their_second = lax.dynamic_index_in_dim(second, 1 - panel, 0, keepdims=False)
    their_tile = lax.dynamic_index_in_dim(strip_tile, 1 - panel, 0, keepdims=False)
    mine = jnp.stack([jnp.where((theirs == me) & (their_second == h), 1, 0) for h in range(2)])
    ids = jnp.sum(mine * order, axis=1)
    tiles = jnp.sum(mine[:, :, None] * their_tile.reshape(1, pairs, 2), axis=1).reshape(4)
    info = jnp.concatenate([ids, tiles, jnp.zeros((2,), jnp.int32)]).astype(jnp.int32)
    f32 = jnp.float32
    vm = pltpu.VMEM
    dma = pltpu.SemaphoreType.DMA
    devices = lat_n * lon_n
    tiles_out = 4 * lon_n + 2 * lat_n
    anywhere = pl.BlockSpec(memory_space=pl.ANY)
    smem = pl.BlockSpec(memory_space=pltpu.SMEM)
    out = pl.pallas_call(
        functools.partial(kernel, lat_n, lon_n),
        out_shape=jax.ShapeDtypeStruct((FIELDS, ROWS, COLS), f32),
        in_specs=[smem, smem, anywhere, anywhere, anywhere, anywhere],
        out_specs=anywhere,
        scratch_shapes=[
            vm((FIELDS, TALL, COLS), f32),
            vm((FIELDS, TALL, COLS), f32),
            vm((LEVELS, ROWS, COLS), f32),
            vm((LEVELS, TALL, COLS), f32),
            vm((LEVELS + 1, ROWS, COLS), f32),
            vm((LEVELS, 10, ROWS, COLS), f32),
            vm((LEVELS + 1, ROWS, COLS), f32),
            vm(weights.shape[1:], weights.dtype),
            vm((128, 256), f32),
            vm((STEPS, 4, ROWS, COLS), f32),
            vm((STEPS, 2, 4, ROWS, COLS), f32),
            vm((4, ROWS, COLS), f32),
            vm((STEPS, 2, FIELDS + LEVELS, 2, COLS), f32),
            vm((STEPS, 2, FIELDS + LEVELS, 2, COLS), f32),
            vm((2, ROWS, COLS), f32),
            vm((STEPS, MIDS, SHARE, COLS), f32),
            vm((devices, SHARE, COLS), f32),
            vm((devices, SHARE, COLS), f32),
            vm((STEPS, tiles_out, SHARE, COLS), f32),
            vm((STEPS, MIDS, 2, SHARE, COLS), f32),
            vm((STEPS, MIDS, SHARE, COLS), f32),
            vm((2, 128, COLS), f32),
            vm((128, COLS), f32),
            dma((5,)),
            dma((STEPS, 4)),
            dma((STEPS, 4)),
            dma((STEPS,)),
            dma((STEPS,)),
            dma((STEPS,)),
            dma((STEPS,)),
            dma((STEPS,)),
            dma((STEPS,)),
        ],
        compiler_params=pltpu.CompilerParams(
            collective_id=0, has_side_effects=True, vmem_limit_bytes=56 * 1024 * 1024),
    )(
        tab, info,
        tracers.reshape(FIELDS, ROWS, COLS),
        winds.reshape(2, LEVELS, ROWS, COLS),
        mixing.reshape(LEVELS - 1, ROWS, COLS),
        weights,
    )
    return out.reshape(tracers.shape)


def solution(mesh):
    return jax.shard_map(
        functools.partial(on_device, mesh.shape["lat"], mesh.shape["lon"]),
        mesh=mesh,
        in_specs=(
            P("panel", None, None, "lat", "lon"),
            P("panel", None, None, "lat", "lon"),
            P("panel", None, "lat", "lon"),
            P(),
            P(),
            P(),
        ),
        out_specs=P("panel", None, None, "lat", "lon"),
        check_vma=False,
    )
```

time: 1110 us -> 110 us (0.10); the launches traced: 1090 us -> 109 us
  waiting for transfers between devices: 410 us -> 0 us
  local copies, waits for them, and re-layouts: 279 us -> 14.6 us
  blocking collectives: 218 us -> 0 us
  other arithmetic: 109 us -> 1.8 us
  Pallas kernels: 0 us -> 93 us
  starting transfers between devices: 66.6 us -> 0 us
    ppermute x14 -> x0, waiting for transfers between devices: 312 us -> none  [the longest x2 310 us: from_partner(): return lax.ppermute(value, axis, pairs)]
    all_to_all x1 -> x0, blocking collectives: 218 us -> none  [on_device(): lax.all_to_all(crossed, ('lat', 'lon'), split_axis=0, concat_axis=0, tile...]
    all_to_all x1 -> x0, waiting for transfers between devices: 98.7 us -> none  [on_device(): lax.all_to_all(crossed, ('lat', 'lon'), split_axis=0, concat_axis=0, tile...]
    pallas_call x0 -> x1, Pallas kernels: none -> 93 us  [on_device(): pl.pallas_call(functools.partial(kernel, lat_n, lon_n), out_shape=jax.Sha...]
    reshape x21 -> x1, local copies, waits for them, and re-layouts: 60.3 us -> 0.08 us  [on_device(): jnp.sum(mine[:, :, None] * their_tile.reshape(1, pairs, 2), axis=1)]
    gather x14 -> x0, local copies, waits for them, and re-layouts: 58.9 us -> none  [the longest x4 29.4 us: on_device(): picked = jnp.take(tile_table, send_tile, axis=0)]
    ppermute x14 -> x0, starting transfers between devices: 51.6 us -> none  [the longest x6 32.4 us: with_halo(): before = lax.ppermute(last, axis, up)]
    slice x17 -> x1, local copies, waits for them, and re-layouts: 32.8 us -> 0.91 us  [on_device(): sources = strip_source[:, ::2]]
  transfers between devices with their start and end apart: 15 -> 0, of which waited for: 5 -> 0; matrix products, arithmetic and copies ran while one was open for 9% -> 0% of each run, Pallas kernels for 0% -> 0%
where the time goes in v1:
time: 110 us; the launch traced here: 109 us
  Pallas kernels  93 us (85%)
  local copies, waits for them, and re-layouts  14.6 us (13%)
  other arithmetic  1.8 us (2%)
    pallas_call x1, Pallas kernels, on_device(): pl.pallas_call(functools.partial(kernel, lat_n, lon_n), out_shape=jax.Sha...  93 us
    unnamed x4, local copies, waits for them, and re-layouts  13.4 us

profile of v1, /device:TPU:1, one launch (start us, length us, event | category | flops | bytes accessed | tf_op | source)
XLA Modules:
  0.0 109.5 jit_solution(4648659704718105125)
XLA Ops:
  0.0 0.0 copy-start
  0.0 0.9 slice.3
  0.9 0.0 copy-done
  1.0 0.3 and_reduce_fusion
  1.2 0.6 and_select_fusion.1
  1.8 0.1 multiply_reduce_fusion.1
  1.9 0.1 mul.38
  2.1 0.1 copy.9
  2.2 0.2 multiply_reduce_fusion
  2.3 0.1 reshape.33
  2.4 0.7 pad_add_fusion.1.info
  3.1 10.0 %copy.10.wt_hbm = bf16[2,320,32,64]{3,2,1,0:T(8,128)(2,1)} copy(bf16[2,320,32,64]{1,3,2,0:T(8,128)(2,1)} %param.11) | data formatting | bytes 5242880 | tf_op args[5]
  13.1 93.0 %shard_map.64 = f32[72,64,128]{2,1,0:T(8,128)} custom-call(s32[160]{0:T(256)} %bitcast.9, s32[8]{0:T(128)} %pad_add_fusion.1.info, f32[72,64,128]{2,1,0:T(8,128)} %bitcast.6, f32[2,36,64,128]{3,2,1,0:T(8,128)} %bitcast.7, f32[35,64,128]{2,1,0:T(8,128)} %bitcast.8, bf16[2,320,32,64]{3,2,1,0:T(8,128)(2,1)} %copy.10.wt_hbm), custom_call_target="tpu_custom_call" | custom-call | tf_op jit(solution)/shard_map/pallas_call | solution.py:462
  106.1 3.4 %copy.12 = f32[1,2,36,64,128]{4,3,2,1,0:T(8,128)} copy(f32[1,2,36,64,128]{4,3,2,1,0:T(8,128)} %bitcast.5) | data formatting | bytes 4718592
  (4 shorter events, 0.1 us)
Async XLA Ops:
  0.0 0.9 copy-start
